TPU v7x, 32 devices: a whole 2x2x4 slice. The times are simulated.
32 devices in a mesh: gx: 4 (over y, x), gy: 4 (over z), gz: 2 (over core).
Axes of the slice: x: 2, y: 2, z: 4, core: 2. Of those that a mesh axis runs over, the one named last changes fastest.
Arguments:
- displacement: bfloat16 [4, 4, 2, 768, 128], P('gx', 'gy', 'gz'), may hold values from -6 to 6
- flexibility: bfloat16 [4, 4, 2, 768, 768], P('gx', 'gy', 'gz'), as said below
- schur: bfloat16 [4, 4, 2, 768, 768], P('gx', 'gy', 'gz'), as said below
- face_rows: int32 [4, 4, 2, 768], P('gx', 'gy', 'gz'), may hold values from 0 to 767, as said below
- multiplicity: int32 [4, 4, 2, 768], P('gx', 'gy', 'gz'), may hold values from 2 to 8, as said below
Outputs:
- multipliers: float32 [4, 4, 2, 768, 128], P('gx', 'gy', 'gz')
Inputs may be any that keep to these rules, and one draw needn't show every extreme that they name: `flexibility`: symmetric and positive definite. `schur`: symmetric and positive definite. `face_rows`: an interface unknown may be constrained by several slots of its subdomain. `multiplicity`: each value is 2, 4 or 8; a slot and its partner slot carry the same value.
All inputs are finite; a program needn't handle non-finite values.
Results may differ from a plain program's by a relative error of at most 0.017.
Values may be sent and summed in bfloat16 or wider, within the bound.
A program may use at most 64 MiB of HBM per device.

v0:
```python
import jax
import jax.numpy as jnp
from jax import lax
from jax.sharding import PartitionSpec as P

ITERS = 3


def padded(value, sides, width):
    for axis, dim in sides:
        devices, length = (lax.axis_size(axis), value.shape[dim])
        up = [(i, (i + 1) % devices) for i in range(devices - 1)]
        down = [(j, i) for i, j in up]
        last = lax.slice_in_dim(value, length - width, length, axis=dim)
        initial = lax.slice_in_dim(value, 0, width, axis=dim)
        before = lax.ppermute(last, axis, up)
        after = lax.ppermute(initial, axis, down)
        value = jnp.concatenate([before, value, after], axis=dim)
    return value


def shards(displacement, flexibility, schur, face_rows, multiplicity):
    width = flexibility.shape[-1]
    loads = displacement.shape[-1]
    slots = face_rows.shape[-1]
    face_len = slots // 6
    displaced = displacement.reshape(width, loads)
    flex_op = flexibility.reshape(width, width)
    schur_op = schur.reshape(width, width)
    row_list = face_rows.reshape(slots)
    weight = 2.0 / multiplicity.reshape(slots, 1).astype(jnp.float32)
    index_x = lax.axis_index("gx")
    index_y = lax.axis_index("gy")
    index_z = lax.axis_index("gz")
    have = jnp.stack(
        [
            index_x > 0,
            index_x < lax.axis_size("gx") - 1,
            index_y > 0,
            index_y < lax.axis_size("gy") - 1,
            index_z > 0,
            index_z < lax.axis_size("gz") - 1,
        ]
    )
    inner = jnp.repeat(jnp.where(have, 0.5, 1.0).astype(jnp.float32), face_len).reshape(slots, 1)
    columns = jnp.arange(width, dtype=jnp.int32).reshape(1, width)
    pick_table = (row_list.reshape(slots, 1) == columns).astype(jnp.bfloat16)
    spread_table = (row_list.reshape(slots, 1) == columns).astype(jnp.float32).T

    def own_faces(values):
        return jnp.dot(pick_table, values, preferred_element_type=jnp.float32).reshape(
            6, face_len, loads
        )

    lists = padded(row_list.reshape(1, 1, 1, 6, face_len), (("gx", 0), ("gy", 1), ("gz", 2)), 1)
    partner_rows = jnp.stack(
        [
            lists[0, 1, 1, 1],
            lists[2, 1, 1, 0],
            lists[1, 0, 1, 3],
            lists[1, 2, 1, 2],
            lists[1, 1, 0, 5],
            lists[1, 1, 2, 4],
        ]
    )
    partner_table = (partner_rows.reshape(6, face_len, 1) == columns.reshape(1, 1, width)).astype(
        jnp.bfloat16
    )

    def jump(values):
        block = values.reshape(1, width, loads)
        near_x = padded(block, (("gx", 0),), 1)
        near_y = padded(block, (("gy", 0),), 1)
        near_z = padded(block, (("gz", 0),), 1)
        beside = jnp.stack([near_x[0], near_x[2], near_y[0], near_y[2], near_z[0], near_z[2]])
        partner = jnp.einsum(
            "ftn,fnl->ftl", partner_table, beside, preferred_element_type=jnp.float32
        )
        own = own_faces(values)
        return (own - partner).reshape(slots, loads)

    def spread(values):
        return jnp.dot(
            spread_table,
            values,
            precision=lax.Precision.HIGHEST,
            preferred_element_type=jnp.float32,
        ).astype(jnp.bfloat16)

    def flex_apply(values):
        return jump(
            jnp.dot(flex_op, spread(values), preferred_element_type=jnp.float32).astype(
                jnp.bfloat16
            )
        )

    def precondition(values):
        return weight * jump(
            jnp.dot(schur_op, spread(weight * values), preferred_element_type=jnp.float32).astype(
                jnp.bfloat16
            )
        )

    def local_inner(left, right):
        return jnp.sum(inner * left * right, axis=0)

    residual = jump(displaced)
    solution = jnp.zeros((slots, loads), jnp.float32)

    def pair_totals(res_now, smooth_now, image_now):
        return lax.psum(
            (local_inner(res_now, smooth_now), local_inner(smooth_now, image_now)),
            ("gx", "gy", "gz"),
        )

    smoothed = precondition(residual)
    image_z = flex_apply(smoothed)
    rho_now, curvature = pair_totals(residual, smoothed, image_z)
    step_len = rho_now / curvature
    direction = smoothed
    along = image_z
    for iteration in range(ITERS):
        solution = solution + step_len * direction
        residual = residual - step_len * along
        if iteration + 1 < ITERS:
            smoothed = precondition(residual)
            image_z = flex_apply(smoothed)
            rho_next, curvature = pair_totals(residual, smoothed, image_z)
            ratio = rho_next / rho_now
            step_len = rho_next / (curvature - ratio * rho_next / step_len)
            direction = smoothed + ratio * direction
            along = image_z + ratio * along
            rho_now = rho_next
    return solution.reshape(1, 1, 1, slots, loads)


def solution(mesh):
    placed = (
        P("gx", "gy", "gz", None, None),
        P("gx", "gy", "gz", None, None),
        P("gx", "gy", "gz", None, None),
        P("gx", "gy", "gz", None),
        P("gx", "gy", "gz", None),
    )
    return jax.shard_map(
        shards,
        mesh=mesh,
        in_specs=placed,
        out_specs=P("gx", "gy", "gz", None, None),
        check_vma=False,
    )
```

profile of v0, /device:TPU:0, one launch (start us, length us, event | category | flops | bytes accessed | tf_op | source)
XLA Modules:
  0.0 294.6 jit_solution(12174385282993255522)
XLA Ops:
  0.8 4.8 %collective-permute-start = (s32[1,1,1,6,128]{4,3,2,1,0:T(8,128)S(1)}, s32[1,1,1,6,128]{4,3,2,1,0:T(8,128)S(1)}, u32[]{:S(2)}, u32[]{:S(2)}) collective-permute-start(s32[1,1,1,6,128]{4,3,2,1,0:T(8,128)S(1)} %bitcast.178), channel_id=1, source_target_pairs={{0,8},{8,16},{16,24},{1,9},{9,17},{17,25},{2,10},{10,18},{18,26},{... | collective-permute-start | bytes 9224 | tf_op jit(solution)/shard_map/ppermute | solution.py:16
  7.0 4.6 %collective-permute-start.6 = (bf16[1,768,128]{2,1,0:T(8,128)(2,1)}, bf16[1,768,128]{2,1,0:T(8,128)(2,1)S(1)}, u32[]{:S(2)}, u32[]{:S(2)}) collective-permute-start(bf16[1,768,128]{2,1,0:T(8,128)(2,1)} %bitcast.183), channel_id=1, source_target_pairs={{0,8},{8,16},{16,24},{1,9},{9,17},{17,25},{2,10},{10,18},{18,26},{... | collective-permute-start | bytes 589832 | tf_op jit(solution)/shard_map/ppermute | solution.py:16
  12.8 3.5 %collective-permute-start.8 = (bf16[1,768,128]{2,1,0:T(8,128)(2,1)}, bf16[1,768,128]{2,1,0:T(8,128)(2,1)S(1)}, u32[]{:S(2)}, u32[]{:S(2)}) collective-permute-start(bf16[1,768,128]{2,1,0:T(8,128)(2,1)} %bitcast.185), channel_id=1, source_target_pairs={{0,2},{2,4},{4,6},{1,3},{3,5},{5,7},{8,10},{10,12},{12,14},{9,11},... | collective-permute-start | bytes 589832 | tf_op jit(solution)/shard_map/ppermute | solution.py:16
  18.1 3.5 %collective-permute-start.2 = (s32[3,1,1,6,128]{4,3,2,1,0:T(8,128)S(1)}, s32[3,1,1,6,128]{4,3,2,1,0:T(8,128)S(1)}, u32[]{:S(2)}, u32[]{:S(2)}) collective-permute-start(s32[3,1,1,6,128]{4,3,2,1,0:T(8,128)S(1)} %pad_add_fusion.1), channel_id=1, source_target_pairs={{0,2},{2,4},{4,6},{1,3},{3,5},{5,7},{8,10},{10,12},{12,14},{9,11},... | collective-permute-start | bytes 27656 | tf_op jit(solution)/shard_map/ppermute | solution.py:16
  24.2 3.0 %collective-permute-done.3 = s32[3,1,1,6,128]{4,3,2,1,0:T(8,128)S(1)} collective-permute-done((s32[3,1,1,6,128]{4,3,2,1,0:T(8,128)S(1)}, s32[3,1,1,6,128]{4,3,2,1,0:T(8,128)S(1)}, u32[]{:S(2)}, u32[]{:S(2)}) %collective-permute-start.3) | collective-permute-done | bytes 9248 | tf_op jit(solution)/shard_map/ppermute | solution.py:17
  30.3 2.1 collective-permute-start.4
  33.2 2.3 collective-permute-start.10
  39.7 2.1 fusion.79
  42.4 4.9 %collective-permute-start.12 = (bf16[1,768,128]{1,2,0:T(8,128)(2,1)S(1)}, bf16[1,768,128]{1,2,0:T(8,128)(2,1)S(1)}, u32[]{:S(2)}, u32[]{:S(2)}) collective-permute-start(bf16[1,768,128]{1,2,0:T(8,128)(2,1)S(1)} %bitcast.148), channel_id=1, source_target_pairs={{0,8},{8,16},{16,24},{1,9},{9,17},{17,25},{2,10},{10,18},{18,26},{... | collective-permute-start | bytes 589832 | tf_op jit(solution)/shard_map/ppermute | solution.py:16
  48.6 3.5 %collective-permute-start.14 = (bf16[1,768,128]{1,2,0:T(8,128)(2,1)S(1)}, bf16[1,768,128]{1,2,0:T(8,128)(2,1)S(1)}, u32[]{:S(2)}, u32[]{:S(2)}) collective-permute-start(bf16[1,768,128]{1,2,0:T(8,128)(2,1)S(1)} %bitcast.150), channel_id=1, source_target_pairs={{0,2},{2,4},{4,6},{1,3},{3,5},{5,7},{8,10},{10,12},{12,14},{9,11},... | collective-permute-start | bytes 589832 | tf_op jit(solution)/shard_map/ppermute | solution.py:16
  56.8 2.6 collective-permute-done.13
  61.2 2.1 fusion.80
  63.9 5.5 %collective-permute-start.18 = (bf16[1,768,128]{1,2,0:T(8,128)(2,1)S(1)}, bf16[1,768,128]{1,2,0:T(8,128)(2,1)S(1)}, u32[]{:S(2)}, u32[]{:S(2)}) collective-permute-start(bf16[1,768,128]{1,2,0:T(8,128)(2,1)S(1)} %bitcast.154), channel_id=1, source_target_pairs={{0,8},{8,16},{16,24},{1,9},{9,17},{17,25},{2,10},{10,18},{18,26},{... | collective-permute-start | bytes 589832 | tf_op jit(solution)/shard_map/ppermute | solution.py:16
  70.7 2.7 collective-permute-start.20
  79.6 2.1 collective-permute-done.21
  82.6 41.9 %all-reduce.2 = (f32[128]{0:T(128)S(1)}, f32[128]{0:T(128)S(1)}) all-reduce(f32[128]{0:T(128)S(1)} %get-tuple-element.10, f32[128]{0:T(128)S(1)} %get-tuple-element.9), channel_id=1, replica_groups=mesh['gx'=4,'gy'=4,'gz'=2] {'gx','gy','gz'}, use_global_device_ids=true, to_apply=%region_1.2 | all-reduce | flops 256 | bytes 2048 | tf_op jit(solution)/shard_map/psum | solution.py:111
  124.6 2.2 fusion.81
  127.4 4.2 %collective-permute-start.24 = (bf16[1,768,128]{1,2,0:T(8,128)(2,1)S(1)}, bf16[1,768,128]{1,2,0:T(8,128)(2,1)S(1)}, u32[]{:S(2)}, u32[]{:S(2)}) collective-permute-start(bf16[1,768,128]{1,2,0:T(8,128)(2,1)S(1)} %bitcast.160), channel_id=1, source_target_pairs={{0,8},{8,16},{16,24},{1,9},{9,17},{17,25},{2,10},{10,18},{18,26},{... | collective-permute-start | bytes 589832 | tf_op jit(solution)/shard_map/ppermute | solution.py:16
  132.9 2.8 collective-permute-start.26
  144.1 2.1 fusion.82
  146.8 4.6 %collective-permute-start.30 = (bf16[1,768,128]{1,2,0:T(8,128)(2,1)S(1)}, bf16[1,768,128]{1,2,0:T(8,128)(2,1)S(1)}, u32[]{:S(2)}, u32[]{:S(2)}) collective-permute-start(bf16[1,768,128]{1,2,0:T(8,128)(2,1)S(1)} %bitcast.166), channel_id=1, source_target_pairs={{0,8},{8,16},{16,24},{1,9},{9,17},{17,25},{2,10},{10,18},{18,26},{... | collective-permute-start | bytes 589832 | tf_op jit(solution)/shard_map/ppermute | solution.py:16
  152.6 3.4 %collective-permute-start.32 = (bf16[1,768,128]{1,2,0:T(8,128)(2,1)S(1)}, bf16[1,768,128]{1,2,0:T(8,128)(2,1)S(1)}, u32[]{:S(2)}, u32[]{:S(2)}) collective-permute-start(bf16[1,768,128]{1,2,0:T(8,128)(2,1)S(1)} %bitcast.168), channel_id=1, source_target_pairs={{0,2},{2,4},{4,6},{1,3},{3,5},{5,7},{8,10},{10,12},{12,14},{9,11},... | collective-permute-start | bytes 589832 | tf_op jit(solution)/shard_map/ppermute | solution.py:16
  161.7 2.7 collective-permute-done.33
  166.4 41.8 %all-reduce.1 = (f32[128]{0:T(128)}, f32[128]{0:T(128)}) all-reduce(f32[128]{0:T(128)} %get-tuple-element.8, f32[128]{0:T(128)} %get-tuple-element.7), channel_id=1, replica_groups=mesh['gx'=4,'gy'=4,'gz'=2] {'gx','gy','gz'}, use_global_device_ids=true, to_apply=%region_5.6 | all-reduce | flops 256 | bytes 2048 | tf_op jit(solution)/shard_map/psum | solution.py:111
  210.7 2.1 fusion.83
  213.4 4.2 %collective-permute-start.36 = (bf16[1,768,128]{1,2,0:T(8,128)(2,1)S(1)}, bf16[1,768,128]{1,2,0:T(8,128)(2,1)S(1)}, u32[]{:S(2)}, u32[]{:S(2)}) collective-permute-start(bf16[1,768,128]{1,2,0:T(8,128)(2,1)S(1)} %bitcast.172), channel_id=1, source_target_pairs={{0,8},{8,16},{16,24},{1,9},{9,17},{17,25},{2,10},{10,18},{18,26},{... | collective-permute-start | bytes 589832 | tf_op jit(solution)/shard_map/ppermute | solution.py:16
  218.9 2.6 collective-permute-start.38
  230.1 2.1 fusion.84
  232.8 4.3 %collective-permute-start.42 = (bf16[1,768,128]{1,2,0:T(8,128)(2,1)S(1)}, bf16[1,768,128]{1,2,0:T(8,128)(2,1)S(1)}, u32[]{:S(2)}, u32[]{:S(2)}) collective-permute-start(bf16[1,768,128]{1,2,0:T(8,128)(2,1)S(1)} %bitcast.142), channel_id=1, source_target_pairs={{0,8},{8,16},{16,24},{1,9},{9,17},{17,25},{2,10},{10,18},{18,26},{... | collective-permute-start | bytes 589832 | tf_op jit(solution)/shard_map/ppermute | solution.py:16
  238.4 3.5 %collective-permute-start.44 = (bf16[1,768,128]{1,2,0:T(8,128)(2,1)S(1)}, bf16[1,768,128]{1,2,0:T(8,128)(2,1)S(1)}, u32[]{:S(2)}, u32[]{:S(2)}) collective-permute-start(bf16[1,768,128]{1,2,0:T(8,128)(2,1)S(1)} %bitcast.144), channel_id=1, source_target_pairs={{0,2},{2,4},{4,6},{1,3},{3,5},{5,7},{8,10},{10,12},{12,14},{9,11},... | collective-permute-start | bytes 589832 | tf_op jit(solution)/shard_map/ppermute | solution.py:16
  247.8 2.4 collective-permute-done.45
  251.0 41.6 %all-reduce = (f32[128]{0:T(128)S(1)}, f32[128]{0:T(128)S(1)}) all-reduce(f32[128]{0:T(128)S(1)} %get-tuple-element.6, f32[128]{0:T(128)S(1)} %get-tuple-element.5), channel_id=1, replica_groups=mesh['gx'=4,'gy'=4,'gz'=2] {'gx','gy','gz'}, use_global_device_ids=true, to_apply=%region_9.10 | all-reduce | flops 256 | bytes 2048 | tf_op jit(solution)/shard_map/psum | solution.py:111
  (192 shorter events, 75.5 us)
Async XLA Ops:
  0.8 17.2 %collective-permute-start = (s32[1,1,1,6,128]{4,3,2,1,0:T(8,128)S(1)}, s32[1,1,1,6,128]{4,3,2,1,0:T(8,128)S(1)}, u32[]{:S(2)}, u32[]{:S(2)}) collective-permute-start(s32[1,1,1,6,128]{4,3,2,1,0:T(8,128)S(1)} %bitcast.178), channel_id=1, source_target_pairs={{0,8},{8,16},{16,24},{1,9},{9,17},{17,25},{2,10},{10,18},{18,26},{... | collective-permute-start | bytes 9224 | tf_op jit(solution)/shard_map/ppermute | solution.py:16
  5.7 12.4 %collective-permute-start.1 = (s32[1,1,1,6,128]{4,3,2,1,0:T(8,128)S(1)}, s32[1,1,1,6,128]{4,3,2,1,0:T(8,128)S(1)}, u32[]{:S(2)}, u32[]{:S(2)}) collective-permute-start(s32[1,1,1,6,128]{4,3,2,1,0:T(8,128)S(1)} %bitcast.179), channel_id=1, source_target_pairs={{8,0},{16,8},{24,16},{9,1},{17,9},{25,17},{10,2},{18,10},{26,18},{... | collective-permute-start | bytes 9224 | tf_op jit(solution)/shard_map/ppermute | solution.py:17
  7.0 28.5 %collective-permute-start.6 = (bf16[1,768,128]{2,1,0:T(8,128)(2,1)}, bf16[1,768,128]{2,1,0:T(8,128)(2,1)S(1)}, u32[]{:S(2)}, u32[]{:S(2)}) collective-permute-start(bf16[1,768,128]{2,1,0:T(8,128)(2,1)} %bitcast.183), channel_id=1, source_target_pairs={{0,8},{8,16},{16,24},{1,9},{9,17},{17,25},{2,10},{10,18},{18,26},{... | collective-permute-start | bytes 589832 | tf_op jit(solution)/shard_map/ppermute | solution.py:16
  11.5 25.3 %collective-permute-start.7 = (bf16[1,768,128]{2,1,0:T(8,128)(2,1)}, bf16[1,768,128]{2,1,0:T(8,128)(2,1)S(1)}, u32[]{:S(2)}, u32[]{:S(2)}) collective-permute-start(bf16[1,768,128]{2,1,0:T(8,128)(2,1)} %bitcast.184), channel_id=1, source_target_pairs={{8,0},{16,8},{24,16},{9,1},{17,9},{25,17},{10,2},{18,10},{26,18},{... | collective-permute-start | bytes 589832 | tf_op jit(solution)/shard_map/ppermute | solution.py:17
  12.8 24.1 %collective-permute-start.8 = (bf16[1,768,128]{2,1,0:T(8,128)(2,1)}, bf16[1,768,128]{2,1,0:T(8,128)(2,1)S(1)}, u32[]{:S(2)}, u32[]{:S(2)}) collective-permute-start(bf16[1,768,128]{2,1,0:T(8,128)(2,1)} %bitcast.185), channel_id=1, source_target_pairs={{0,2},{2,4},{4,6},{1,3},{3,5},{5,7},{8,10},{10,12},{12,14},{9,11},... | collective-permute-start | bytes 589832 | tf_op jit(solution)/shard_map/ppermute | solution.py:16
  23.0 14.0 %collective-permute-start.9 = (bf16[1,768,128]{2,1,0:T(8,128)(2,1)S(1)}, bf16[1,768,128]{2,1,0:T(8,128)(2,1)S(1)}, u32[]{:S(2)}, u32[]{:S(2)}) collective-permute-start(bf16[1,768,128]{2,1,0:T(8,128)(2,1)S(1)} %bitcast.186), channel_id=1, source_target_pairs={{2,0},{4,2},{6,4},{3,1},{5,3},{7,5},{10,8},{12,10},{14,12},{11,9},... | collective-permute-start | bytes 589832 | tf_op jit(solution)/shard_map/ppermute | solution.py:17
  42.4 13.1 %collective-permute-start.12 = (bf16[1,768,128]{1,2,0:T(8,128)(2,1)S(1)}, bf16[1,768,128]{1,2,0:T(8,128)(2,1)S(1)}, u32[]{:S(2)}, u32[]{:S(2)}) collective-permute-start(bf16[1,768,128]{1,2,0:T(8,128)(2,1)S(1)} %bitcast.148), channel_id=1, source_target_pairs={{0,8},{8,16},{16,24},{1,9},{9,17},{17,25},{2,10},{10,18},{18,26},{... | collective-permute-start | bytes 589832 | tf_op jit(solution)/shard_map/ppermute | solution.py:16
  47.3 12.1 %collective-permute-start.13 = (bf16[1,768,128]{1,2,0:T(8,128)(2,1)S(1)}, bf16[1,768,128]{1,2,0:T(8,128)(2,1)S(1)}, u32[]{:S(2)}, u32[]{:S(2)}) collective-permute-start(bf16[1,768,128]{1,2,0:T(8,128)(2,1)S(1)} %bitcast.149), channel_id=1, source_target_pairs={{8,0},{16,8},{24,16},{9,1},{17,9},{25,17},{10,2},{18,10},{26,18},{... | collective-permute-start | bytes 589832 | tf_op jit(solution)/shard_map/ppermute | solution.py:17
  48.6 10.8 %collective-permute-start.14 = (bf16[1,768,128]{1,2,0:T(8,128)(2,1)S(1)}, bf16[1,768,128]{1,2,0:T(8,128)(2,1)S(1)}, u32[]{:S(2)}, u32[]{:S(2)}) collective-permute-start(bf16[1,768,128]{1,2,0:T(8,128)(2,1)S(1)} %bitcast.150), channel_id=1, source_target_pairs={{0,2},{2,4},{4,6},{1,3},{3,5},{5,7},{8,10},{10,12},{12,14},{9,11},... | collective-permute-start | bytes 589832 | tf_op jit(solution)/shard_map/ppermute | solution.py:16
  52.1 8.3 %collective-permute-start.15 = (bf16[1,768,128]{1,2,0:T(8,128)(2,1)S(1)}, bf16[1,768,128]{1,2,0:T(8,128)(2,1)S(1)}, u32[]{:S(2)}, u32[]{:S(2)}) collective-permute-start(bf16[1,768,128]{1,2,0:T(8,128)(2,1)S(1)} %bitcast.151), channel_id=1, source_target_pairs={{2,0},{4,2},{6,4},{3,1},{5,3},{7,5},{10,8},{12,10},{14,12},{11,9},... | collective-permute-start | bytes 589832 | tf_op jit(solution)/shard_map/ppermute | solution.py:17
  53.4 7.0 %collective-permute-start.16 = (bf16[1,768,128]{1,2,0:T(8,128)(2,1)S(1)}, bf16[1,768,128]{1,2,0:T(8,128)(2,1)S(1)}, u32[]{:S(2)}, u32[]{:S(2)}) collective-permute-start(bf16[1,768,128]{1,2,0:T(8,128)(2,1)S(1)} %bitcast.152), channel_id=1, source_target_pairs={{0,1},{2,3},{4,5},{6,7},{8,9},{10,11},{12,13},{14,15},{16,17},{18,... | collective-permute-start | bytes 589832 | tf_op jit(solution)/shard_map/ppermute | solution.py:16
  63.9 12.9 %collective-permute-start.18 = (bf16[1,768,128]{1,2,0:T(8,128)(2,1)S(1)}, bf16[1,768,128]{1,2,0:T(8,128)(2,1)S(1)}, u32[]{:S(2)}, u32[]{:S(2)}) collective-permute-start(bf16[1,768,128]{1,2,0:T(8,128)(2,1)S(1)} %bitcast.154), channel_id=1, source_target_pairs={{0,8},{8,16},{16,24},{1,9},{9,17},{17,25},{2,10},{10,18},{18,26},{... | collective-permute-start | bytes 589832 | tf_op jit(solution)/shard_map/ppermute | solution.py:16
  69.4 10.2 %collective-permute-start.19 = (bf16[1,768,128]{1,2,0:T(8,128)(2,1)S(1)}, bf16[1,768,128]{1,2,0:T(8,128)(2,1)S(1)}, u32[]{:S(2)}, u32[]{:S(2)}) collective-permute-start(bf16[1,768,128]{1,2,0:T(8,128)(2,1)S(1)} %bitcast.155), channel_id=1, source_target_pairs={{8,0},{16,8},{24,16},{9,1},{17,9},{25,17},{10,2},{18,10},{26,18},{... | collective-permute-start | bytes 589832 | tf_op jit(solution)/shard_map/ppermute | solution.py:17
  70.7 8.9 %collective-permute-start.20 = (bf16[1,768,128]{1,2,0:T(8,128)(2,1)S(1)}, bf16[1,768,128]{1,2,0:T(8,128)(2,1)S(1)}, u32[]{:S(2)}, u32[]{:S(2)}) collective-permute-start(bf16[1,768,128]{1,2,0:T(8,128)(2,1)S(1)} %bitcast.156), channel_id=1, source_target_pairs={{0,2},{2,4},{4,6},{1,3},{3,5},{5,7},{8,10},{10,12},{12,14},{9,11},... | collective-permute-start | bytes 589832 | tf_op jit(solution)/shard_map/ppermute | solution.py:16
  73.4 8.3 %collective-permute-start.21 = (bf16[1,768,128]{1,2,0:T(8,128)(2,1)S(1)}, bf16[1,768,128]{1,2,0:T(8,128)(2,1)S(1)}, u32[]{:S(2)}, u32[]{:S(2)}) collective-permute-start(bf16[1,768,128]{1,2,0:T(8,128)(2,1)S(1)} %bitcast.157), channel_id=1, source_target_pairs={{2,0},{4,2},{6,4},{3,1},{5,3},{7,5},{10,8},{12,10},{14,12},{11,9},... | collective-permute-start | bytes 589832 | tf_op jit(solution)/shard_map/ppermute | solution.py:17
  127.4 11.5 %collective-permute-start.24 = (bf16[1,768,128]{1,2,0:T(8,128)(2,1)S(1)}, bf16[1,768,128]{1,2,0:T(8,128)(2,1)S(1)}, u32[]{:S(2)}, u32[]{:S(2)}) collective-permute-start(bf16[1,768,128]{1,2,0:T(8,128)(2,1)S(1)} %bitcast.160), channel_id=1, source_target_pairs={{0,8},{8,16},{16,24},{1,9},{9,17},{17,25},{2,10},{10,18},{18,26},{... | collective-permute-start | bytes 589832 | tf_op jit(solution)/shard_map/ppermute | solution.py:16
  131.6 9.9 %collective-permute-start.25 = (bf16[1,768,128]{1,2,0:T(8,128)(2,1)S(1)}, bf16[1,768,128]{1,2,0:T(8,128)(2,1)S(1)}, u32[]{:S(2)}, u32[]{:S(2)}) collective-permute-start(bf16[1,768,128]{1,2,0:T(8,128)(2,1)S(1)} %bitcast.161), channel_id=1, source_target_pairs={{8,0},{16,8},{24,16},{9,1},{17,9},{25,17},{10,2},{18,10},{26,18},{... | collective-permute-start | bytes 589832 | tf_op jit(solution)/shard_map/ppermute | solution.py:17
  132.9 8.6 %collective-permute-start.26 = (bf16[1,768,128]{1,2,0:T(8,128)(2,1)S(1)}, bf16[1,768,128]{1,2,0:T(8,128)(2,1)S(1)}, u32[]{:S(2)}, u32[]{:S(2)}) collective-permute-start(bf16[1,768,128]{1,2,0:T(8,128)(2,1)S(1)} %bitcast.162), channel_id=1, source_target_pairs={{0,2},{2,4},{4,6},{1,3},{3,5},{5,7},{8,10},{10,12},{12,14},{9,11},... | collective-permute-start | bytes 589832 | tf_op jit(solution)/shard_map/ppermute | solution.py:16
  135.7 7.6 %collective-permute-start.27 = (bf16[1,768,128]{1,2,0:T(8,128)(2,1)S(1)}, bf16[1,768,128]{1,2,0:T(8,128)(2,1)S(1)}, u32[]{:S(2)}, u32[]{:S(2)}) collective-permute-start(bf16[1,768,128]{1,2,0:T(8,128)(2,1)S(1)} %bitcast.163), channel_id=1, source_target_pairs={{2,0},{4,2},{6,4},{3,1},{5,3},{7,5},{10,8},{12,10},{14,12},{11,9},... | collective-permute-start | bytes 589832 | tf_op jit(solution)/shard_map/ppermute | solution.py:17
  146.8 12.7 %collective-permute-start.30 = (bf16[1,768,128]{1,2,0:T(8,128)(2,1)S(1)}, bf16[1,768,128]{1,2,0:T(8,128)(2,1)S(1)}, u32[]{:S(2)}, u32[]{:S(2)}) collective-permute-start(bf16[1,768,128]{1,2,0:T(8,128)(2,1)S(1)} %bitcast.166), channel_id=1, source_target_pairs={{0,8},{8,16},{16,24},{1,9},{9,17},{17,25},{2,10},{10,18},{18,26},{... | collective-permute-start | bytes 589832 | tf_op jit(solution)/shard_map/ppermute | solution.py:16
  151.3 10.3 %collective-permute-start.31 = (bf16[1,768,128]{1,2,0:T(8,128)(2,1)S(1)}, bf16[1,768,128]{1,2,0:T(8,128)(2,1)S(1)}, u32[]{:S(2)}, u32[]{:S(2)}) collective-permute-start(bf16[1,768,128]{1,2,0:T(8,128)(2,1)S(1)} %bitcast.167), channel_id=1, source_target_pairs={{8,0},{16,8},{24,16},{9,1},{17,9},{25,17},{10,2},{18,10},{26,18},{... | collective-permute-start | bytes 589832 | tf_op jit(solution)/shard_map/ppermute | solution.py:17
  152.6 9.1 %collective-permute-start.32 = (bf16[1,768,128]{1,2,0:T(8,128)(2,1)S(1)}, bf16[1,768,128]{1,2,0:T(8,128)(2,1)S(1)}, u32[]{:S(2)}, u32[]{:S(2)}) collective-permute-start(bf16[1,768,128]{1,2,0:T(8,128)(2,1)S(1)} %bitcast.168), channel_id=1, source_target_pairs={{0,2},{2,4},{4,6},{1,3},{3,5},{5,7},{8,10},{10,12},{12,14},{9,11},... | collective-permute-start | bytes 589832 | tf_op jit(solution)/shard_map/ppermute | solution.py:16
  156.1 8.3 %collective-permute-start.33 = (bf16[1,768,128]{1,2,0:T(8,128)(2,1)S(1)}, bf16[1,768,128]{1,2,0:T(8,128)(2,1)S(1)}, u32[]{:S(2)}, u32[]{:S(2)}) collective-permute-start(bf16[1,768,128]{1,2,0:T(8,128)(2,1)S(1)} %bitcast.169), channel_id=1, source_target_pairs={{2,0},{4,2},{6,4},{3,1},{5,3},{7,5},{10,8},{12,10},{14,12},{11,9},... | collective-permute-start | bytes 589832 | tf_op jit(solution)/shard_map/ppermute | solution.py:17
  157.4 7.0 %collective-permute-start.34 = (bf16[1,768,128]{1,2,0:T(8,128)(2,1)S(1)}, bf16[1,768,128]{1,2,0:T(8,128)(2,1)S(1)}, u32[]{:S(2)}, u32[]{:S(2)}) collective-permute-start(bf16[1,768,128]{1,2,0:T(8,128)(2,1)S(1)} %bitcast.170), channel_id=1, source_target_pairs={{0,1},{2,3},{4,5},{6,7},{8,9},{10,11},{12,13},{14,15},{16,17},{18,... | collective-permute-start | bytes 589832 | tf_op jit(solution)/shard_map/ppermute | solution.py:16
  213.4 11.3 %collective-permute-start.36 = (bf16[1,768,128]{1,2,0:T(8,128)(2,1)S(1)}, bf16[1,768,128]{1,2,0:T(8,128)(2,1)S(1)}, u32[]{:S(2)}, u32[]{:S(2)}) collective-permute-start(bf16[1,768,128]{1,2,0:T(8,128)(2,1)S(1)} %bitcast.172), channel_id=1, source_target_pairs={{0,8},{8,16},{16,24},{1,9},{9,17},{17,25},{2,10},{10,18},{18,26},{... | collective-permute-start | bytes 589832 | tf_op jit(solution)/shard_map/ppermute | solution.py:16
  217.6 10.1 %collective-permute-start.37 = (bf16[1,768,128]{1,2,0:T(8,128)(2,1)S(1)}, bf16[1,768,128]{1,2,0:T(8,128)(2,1)S(1)}, u32[]{:S(2)}, u32[]{:S(2)}) collective-permute-start(bf16[1,768,128]{1,2,0:T(8,128)(2,1)S(1)} %bitcast.173), channel_id=1, source_target_pairs={{8,0},{16,8},{24,16},{9,1},{17,9},{25,17},{10,2},{18,10},{26,18},{... | collective-permute-start | bytes 589832 | tf_op jit(solution)/shard_map/ppermute | solution.py:17
  218.9 8.8 %collective-permute-start.38 = (bf16[1,768,128]{1,2,0:T(8,128)(2,1)S(1)}, bf16[1,768,128]{1,2,0:T(8,128)(2,1)S(1)}, u32[]{:S(2)}, u32[]{:S(2)}) collective-permute-start(bf16[1,768,128]{1,2,0:T(8,128)(2,1)S(1)} %bitcast.174), channel_id=1, source_target_pairs={{0,2},{2,4},{4,6},{1,3},{3,5},{5,7},{8,10},{10,12},{12,14},{9,11},... | collective-permute-start | bytes 589832 | tf_op jit(solution)/shard_map/ppermute | solution.py:16
  221.5 7.8 %collective-permute-start.39 = (bf16[1,768,128]{1,2,0:T(8,128)(2,1)S(1)}, bf16[1,768,128]{1,2,0:T(8,128)(2,1)S(1)}, u32[]{:S(2)}, u32[]{:S(2)}) collective-permute-start(bf16[1,768,128]{1,2,0:T(8,128)(2,1)S(1)} %bitcast.175), channel_id=1, source_target_pairs={{2,0},{4,2},{6,4},{3,1},{5,3},{7,5},{10,8},{12,10},{14,12},{11,9},... | collective-permute-start | bytes 589832 | tf_op jit(solution)/shard_map/ppermute | solution.py:17
  232.8 12.4 %collective-permute-start.42 = (bf16[1,768,128]{1,2,0:T(8,128)(2,1)S(1)}, bf16[1,768,128]{1,2,0:T(8,128)(2,1)S(1)}, u32[]{:S(2)}, u32[]{:S(2)}) collective-permute-start(bf16[1,768,128]{1,2,0:T(8,128)(2,1)S(1)} %bitcast.142), channel_id=1, source_target_pairs={{0,8},{8,16},{16,24},{1,9},{9,17},{17,25},{2,10},{10,18},{18,26},{... | collective-permute-start | bytes 589832 | tf_op jit(solution)/shard_map/ppermute | solution.py:16
  237.1 10.6 %collective-permute-start.43 = (bf16[1,768,128]{1,2,0:T(8,128)(2,1)S(1)}, bf16[1,768,128]{1,2,0:T(8,128)(2,1)S(1)}, u32[]{:S(2)}, u32[]{:S(2)}) collective-permute-start(bf16[1,768,128]{1,2,0:T(8,128)(2,1)S(1)} %bitcast.143), channel_id=1, source_target_pairs={{8,0},{16,8},{24,16},{9,1},{17,9},{25,17},{10,2},{18,10},{26,18},{... | collective-permute-start | bytes 589832 | tf_op jit(solution)/shard_map/ppermute | solution.py:17
  238.4 9.3 %collective-permute-start.44 = (bf16[1,768,128]{1,2,0:T(8,128)(2,1)S(1)}, bf16[1,768,128]{1,2,0:T(8,128)(2,1)S(1)}, u32[]{:S(2)}, u32[]{:S(2)}) collective-permute-start(bf16[1,768,128]{1,2,0:T(8,128)(2,1)S(1)} %bitcast.144), channel_id=1, source_target_pairs={{0,2},{2,4},{4,6},{1,3},{3,5},{5,7},{8,10},{10,12},{12,14},{9,11},... | collective-permute-start | bytes 589832 | tf_op jit(solution)/shard_map/ppermute | solution.py:16
  241.9 8.3 %collective-permute-start.45 = (bf16[1,768,128]{1,2,0:T(8,128)(2,1)S(1)}, bf16[1,768,128]{1,2,0:T(8,128)(2,1)S(1)}, u32[]{:S(2)}, u32[]{:S(2)}) collective-permute-start(bf16[1,768,128]{1,2,0:T(8,128)(2,1)S(1)} %bitcast.145), channel_id=1, source_target_pairs={{2,0},{4,2},{6,4},{3,1},{5,3},{7,5},{10,8},{12,10},{14,12},{11,9},... | collective-permute-start | bytes 589832 | tf_op jit(solution)/shard_map/ppermute | solution.py:17
  (33 other events, 497.6 us)
where the time goes:
time: 296 us; the launch traced here: 295 us
  blocking collectives  125 us (42%)
  starting transfers between devices  107 us (36%)
  waiting for transfers between devices  27.8 us (9%)
  matrix products  26.8 us (9%)
  other arithmetic  5.98 us (2%)
    psum x3, blocking collectives, pair_totals(): lax.psum((local_inner(res_now, smooth_now), local_inner(smooth_now, image...  125 us
    ppermute x24, starting transfers between devices, padded(): before = lax.ppermute(last, axis, up)  75.4 us
    ppermute x24, starting transfers between devices, padded(): after = lax.ppermute(initial, axis, down)  31.1 us
    ppermute x24, waiting for transfers between devices, padded(): after = lax.ppermute(initial, axis, down)  26.8 us
    dot_general x6, matrix products, spread(): jnp.dot(spread_table, values, precision=lax.Precision.HIGHEST, preferred_...  13 us
  transfers between devices with their start and end apart: 48, of which 17 were waited for; matrix products, arithmetic and copies ran while one was open for 2% of the time, Pallas kernels for 0%

commit v1 on v0

v1 whole, which is shorter than its diff:
```python
import functools

import jax
import jax.numpy as jnp
from jax import lax
from jax.experimental import pallas as pl
from jax.experimental.pallas import tpu as pltpu
from jax.sharding import PartitionSpec as P

ITERS = 3
AXES = ("gx", "gy", "gz")
STAGES = ("gz", "gy", "gx")
MESH = pl.DeviceIdType.MESH
F32 = jnp.float32
BF16 = jnp.bfloat16


def dot(a, b):
    return jnp.dot(a, b, preferred_element_type=F32)


def kernel(sizes, disp, flex, schur, rows, mult, out, table, picks, wpicks, temp,
           op_a, op_b, send, recv, res, smo, img, along, across, way, vec, red_out, red_in,
           send_sem, recv_sem, red_send_sem, red_recv_sem):
    width, loads = disp.shape
    faces, length = rows.shape
    slots = faces * length
    index = {a: lax.axis_index(a) for a in AXES}
    barrier = pltpu.get_barrier_semaphore()
    peers = 0
    for a in AXES:
        for d in range(1, sizes[a]):
            pl.semaphore_signal(barrier, inc=1, device_id={a: lax.rem(index[a] + d, sizes[a])},
                                device_id_type=MESH)
            peers += 1

    have, toward = [], []
    for a in AXES:
        have += [index[a] > 0, index[a] < sizes[a] - 1]
        toward += [{a: lax.rem(index[a] + sizes[a] - 1, sizes[a])},
                   {a: lax.rem(index[a] + 1, sizes[a])}]
    half = [jnp.where(h, 0.5, 1.0).astype(F32) for h in have]

    def block(f):
        return slice(f * length, (f + 1) * length)

    exchanges = send.shape[0]
    for f in range(faces):
        @pl.when(jnp.logical_not(have[f]))
        def _():
            for e in range(exchanges):
                recv[e, f] = jnp.zeros((length, loads), BF16)

    def face_copy(e, f):
        return pltpu.make_async_remote_copy(
            src_ref=send.at[e, f], dst_ref=recv.at[e, f ^ 1], send_sem=send_sem.at[e, f],
            recv_sem=recv_sem.at[e, f ^ 1], device_id=toward[f], device_id_type=MESH)

    def face_arrival(e, f):
        return pltpu.make_async_remote_copy(
            src_ref=send.at[e, f], dst_ref=recv.at[e, f], send_sem=send_sem.at[e, f],
            recv_sem=recv_sem.at[e, f], device_id=toward[f], device_id_type=MESH)

    def post(e, f, value):
        send[e, f] = value.astype(BF16)

        @pl.when(have[f])
        def _():
            face_copy(e, f).start()

    def jumped(e, f):
        @pl.when(have[f])
        def _():
            face_arrival(e, f).wait_recv()
        return send[e, f].astype(F32) - recv[e, f].astype(F32)

    def red_copy(k, s, d):
        a = STAGES[s]
        return pltpu.make_async_remote_copy(
            src_ref=red_out.at[k, s], dst_ref=red_in.at[k, s, d - 1],
            send_sem=red_send_sem.at[k, s, d - 1], recv_sem=red_recv_sem.at[k, s, d - 1],
            device_id={a: lax.rem(index[a] + d, sizes[a])}, device_id_type=MESH)

    def red_start(k, s, value):
        red_out[k, s] = value
        for d in range(1, sizes[STAGES[s]]):
            red_copy(k, s, d).start()

    def red_finish(k, s):
        total = red_out[k, s]
        for d in range(1, sizes[STAGES[s]]):
            red_copy(k, s, d).wait_recv()
            total = total + red_in[k, s, d - 1]
        return total

    def pair(first, second):
        line = lax.broadcasted_iota(jnp.int32, (8, loads), 0)
        return jnp.where(line == 0, first, jnp.where(line == 1, second, 0.0))

    def total_of(value):
        return jnp.sum(value, axis=0, keepdims=True)

    lanes = lax.broadcasted_iota(jnp.int32, (length, length), 1)
    lines = lax.broadcasted_iota(jnp.int32, (length, length), 0)
    for f in range(faces):
        row = jnp.broadcast_to(rows[f:f + 1, :], (length, length))
        weight = jnp.broadcast_to(2.0 / mult[f:f + 1, :].astype(F32), (length, length))
        row_t = row.astype(F32).T.astype(jnp.int32)
        weight_t = weight.T
        for c in range(width // length):
            table[block(c), block(f)] = jnp.where(row == lines + c * length, 1.0, 0.0).astype(BF16)
            hit = row_t == lanes + c * length
            picks[block(f), block(c)] = jnp.where(hit, 1.0, 0.0).astype(BF16)
            wpicks[block(f), block(c)] = jnp.where(hit, weight_t, 0.0).astype(BF16)

    pl.semaphore_wait(barrier, peers)
    moved = disp[...]
    for f in range(faces):
        post(0, f, dot(picks[block(f), :], moved))

    def gather(left, op, scale, result):
        @pl.loop(0, width // length)
        def _(i):
            part = pl.ds(pl.multiple_of(i * length, length), length)
            temp[part, :] = dot(op[part, :], table[...]).astype(BF16)

        @pl.loop(0, faces)
        def _(i):
            part = pl.ds(pl.multiple_of(i * length, length), length)
            value = dot(left[part, :], temp[...])
            if scale is not None:
                value = value * scale
            result[part, :] = value.astype(BF16)

    weight_row = jnp.concatenate([2.0 / mult[f:f + 1, :].astype(F32) for f in range(faces)], axis=1)
    gather(wpicks, schur, weight_row, op_b)

    for f in range(faces):
        value = jumped(0, f)
        res[block(f), :] = value
        vec[block(f), :] = value.astype(BF16)
    x = vec[...]
    for f in range(faces):
        post(1, f, dot(op_b[block(f), :], x))
    gather(picks, flex, None, op_a)
    rho = jnp.zeros((1, loads), F32)
    for f in range(faces):
        value = jumped(1, f)
        smo[block(f), :] = value
        vec[block(f), :] = value.astype(BF16)
        rho = rho + half[f] * total_of(res[block(f), :] * value)

    alpha = rho_old = None
    for k in range(ITERS):
        last = k + 1 == ITERS
        e = 2 + 2 * k
        x = vec[...]
        curve = jnp.zeros((1, loads), F32)
        for f in range(faces):
            y = dot(op_a[block(f), :], x)
            if not last:
                post(e, f, y)
            curve = curve + total_of(smo[block(f), :] * y)
        red_start(k, 0, pair(rho, curve))
        if last:
            red_start(k, 1, red_finish(k, 0))
            red_start(k, 2, red_finish(k, 1))
        else:
            for f in range(faces):
                value = jumped(e, f)
                img[block(f), :] = value
                vec[block(f), :] = value.astype(BF16)
            red_start(k, 1, red_finish(k, 0))
            x = vec[...]
            for f in range(faces):
                post(e + 1, f, dot(op_b[block(f), :], x))
            red_start(k, 2, red_finish(k, 1))
        sums = red_finish(k, 2)
        rho_now, curve = sums[0:1, :], sums[1:2, :]
        if k == 0:
            beta = None
            alpha = rho_now / curve
        else:
            beta = rho_now / rho_old
            alpha = rho_now / (curve - beta * rho_now / alpha)
        rho_old = rho_now
        rho = jnp.zeros((1, loads), F32)
        for f in range(faces):
            b = block(f)
            p = smo[b, :] if beta is None else smo[b, :] + beta * way[b, :]
            total = alpha * p if beta is None else out[b, :] + alpha * p
            out[b, :] = total
            if last:
                continue
            way[b, :] = p
            q = jumped(e + 1, f)
            s = img[b, :]
            if beta is not None:
                q = q + beta * across[b, :]
                s = s + beta * along[b, :]
            across[b, :] = q
            along[b, :] = s
            r = res[b, :] - alpha * s
            z = smo[b, :] - alpha * q
            res[b, :] = r
            smo[b, :] = z
            vec[b, :] = z.astype(BF16)
            rho = rho + half[f] * total_of(r * z)

    for f in range(faces):
        @pl.when(have[f])
        def _():
            for e in range(exchanges):
                face_copy(e, f).wait_send()
    for k in range(ITERS):
        for s in range(len(STAGES)):
            for d in range(1, sizes[STAGES[s]]):
                red_copy(k, s, d).wait_send()


def shards(sizes, displacement, flexibility, schur, face_rows, multiplicity):
    width = flexibility.shape[-1]
    loads = displacement.shape[-1]
    slots = face_rows.shape[-1]
    length = slots // 6
    exchanges = 2 * ITERS
    most = max(max(sizes.values()) - 1, 1)
    vmem = pl.BlockSpec(memory_space=pltpu.VMEM)
    state = pltpu.VMEM((slots, loads), F32)
    result = pl.pallas_call(
        functools.partial(kernel, sizes),
        out_shape=jax.ShapeDtypeStruct((slots, loads), F32),
        in_specs=[vmem] * 5,
        out_specs=vmem,
        scratch_shapes=[
            pltpu.VMEM((width, slots), BF16),
            pltpu.VMEM((slots, width), BF16),
            pltpu.VMEM((slots, width), BF16),
            pltpu.VMEM((width, slots), BF16),
            pltpu.VMEM((slots, slots), BF16),
            pltpu.VMEM((slots, slots), BF16),
            pltpu.VMEM((exchanges, 6, length, loads), BF16),
            pltpu.VMEM((exchanges, 6, length, loads), BF16),
            state, state, state, state, state, state,
            pltpu.VMEM((slots, loads), BF16),
            pltpu.VMEM((ITERS, 3, 8, loads), F32),
            pltpu.VMEM((ITERS, 3, most, 8, loads), F32),
            pltpu.SemaphoreType.DMA((exchanges, 6)),
            pltpu.SemaphoreType.DMA((exchanges, 6)),
            pltpu.SemaphoreType.DMA((ITERS, 3, most)),
            pltpu.SemaphoreType.DMA((ITERS, 3, most)),
        ],
        compiler_params=pltpu.CompilerParams(
            collective_id=0, has_side_effects=True, vmem_limit_bytes=44 * 1024 * 1024),
    )(
        displacement.reshape(width, loads),
        flexibility.reshape(width, width),
        schur.reshape(width, width),
        face_rows.reshape(6, length),
        multiplicity.reshape(6, length),
    )
    return result.reshape(1, 1, 1, slots, loads)


def solution(mesh):
    whole = P(*AXES, None, None)
    lists = P(*AXES, None)
    return jax.shard_map(
        functools.partial(shards, {a: mesh.shape[a] for a in AXES}),
        mesh=mesh,
        in_specs=(whole, whole, whole, lists, lists),
        out_specs=whole,
        check_vma=False,
    )
```

time: 296 us -> 51.5 us (0.17)
  blocking collectives: 125 us -> 0 us
  starting transfers between devices: 107 us -> 0 us
  Pallas kernels: 0 us -> 45.6 us
  waiting for transfers between devices: 27.8 us -> 0 us
  matrix products: 26.8 us -> 0 us
  other arithmetic: 5.98 us -> 1.4 us
  local copies, waits for them, and re-layouts: 0.91 us -> 4.21 us
    psum x3 -> x0, blocking collectives: 125 us -> none  [pair_totals(): lax.psum((local_inner(res_now, smooth_now), local_inner(smooth_now, image...]
    ppermute x48 -> x0, starting transfers between devices: 107 us -> none  [the longest x24 75.4 us: padded(): before = lax.ppermute(last, axis, up)]
    pallas_call x0 -> x1, Pallas kernels: none -> 45.6 us  [shards(): pl.pallas_call(functools.partial(kernel, sizes), out_shape=jax.ShapeDtype...]
    ppermute x48 -> x0, waiting for transfers between devices: 27.8 us -> none  [the longest x24 26.8 us: padded(): after = lax.ppermute(initial, axis, down)]
    dot_general x26 -> x0, matrix products: 26.8 us -> none  [the longest x6 13 us: spread(): jnp.dot(spread_table, values, precision=lax.Precision.HIGHEST, preferred_...]
    unnamed x69 -> x7, local copies, waits for them, and re-layouts: 0.63 us -> 4.21 us
  transfers between devices with their start and end apart: 48 -> 0, of which waited for: 17 -> 0; matrix products, arithmetic and copies ran while one was open for 2% -> 0% of each run, Pallas kernels for 0% -> 0%
where the time goes in v1:
time: 51.5 us; the launch traced here: 51.3 us
  Pallas kernels  45.6 us (89%)
  local copies, waits for them, and re-layouts  4.21 us (8%)
  other arithmetic  1.4 us (3%)
    pallas_call x1, Pallas kernels, shards(): pl.pallas_call(functools.partial(kernel, sizes), out_shape=jax.ShapeDtype...  45.6 us
    unnamed x7, local copies, waits for them, and re-layouts  4.21 us
    unnamed x2, other arithmetic  1.4 us

profile of v1, /device:TPU:0, one launch (start us, length us, event | category | flops | bytes accessed | tf_op | source)
XLA Modules:
  0.0 51.3 jit_solution(9815410794295065890)
XLA Ops:
  0.0 0.7 %reduce = s32[768]{0:T(1024)S(1)} reduce(s32[1,1,1,768]{3,2,1,0:T(1,128)} %param.8, s32[]{:T(128)} %constant.5), dimensions={0,1,2}, to_apply=%param.8.reduce_sub_computation | reduce | bytes 6148 | tf_op args[3]
  0.7 0.7 %reduce.1 = s32[768]{0:T(1024)S(1)} reduce(s32[1,1,1,768]{3,2,1,0:T(1,128)} %param.9, s32[]{:T(128)} %constant.5), dimensions={0,1,2}, to_apply=%param.9.reduce_sub_computation | reduce | bytes 6148 | tf_op args[4]
  1.4 0.0 copy-start
  1.4 1.3 %copy-done = bf16[1,1,1,768,768]{4,3,2,1,0:T(8,128)(2,1)S(1)} copy-done((bf16[1,1,1,768,768]{4,3,2,1,0:T(8,128)(2,1)S(1)}, bf16[1,1,1,768,768]{4,3,2,1,0:T(8,128)(2,1)}, u32[]{:S(2)}) %copy-start) | copy-done | bytes 1179672
  2.7 0.0 copy-start.1
  2.7 1.3 %copy-done.1 = bf16[1,1,1,768,768]{4,3,2,1,0:T(8,128)(2,1)S(1)} copy-done((bf16[1,1,1,768,768]{4,3,2,1,0:T(8,128)(2,1)S(1)}, bf16[1,1,1,768,768]{4,3,2,1,0:T(8,128)(2,1)}, u32[]{:S(2)}) %copy-start.1) | copy-done | bytes 1179672
  3.9 0.0 copy-start.2
  4.0 0.9 %copy-done.2 = bf16[1,1,1,768,128]{4,3,2,1,0:T(8,128)(2,1)S(1)} copy-done((bf16[1,1,1,768,128]{4,3,2,1,0:T(8,128)(2,1)S(1)}, bf16[1,1,1,768,128]{4,3,2,1,0:T(8,128)(2,1)}, u32[]{:S(2)}) %copy-start.2) | copy-done | bytes 196632
  4.9 45.6 %shard_map.55 = f32[768,128]{1,0:T(8,128)S(1)} custom-call(bf16[768,128]{1,0:T(8,128)(2,1)S(1)} %bitcast.9, bf16[768,768]{1,0:T(8,128)(2,1)S(1)} %bitcast.7, bf16[768,768]{1,0:T(8,128)(2,1)S(1)} %bitcast.8, s32[6,128]{1,0:T(8,128)S(1)} %bitcast.10, s32[6,128]{1,0:T(8,128)S(1)} %bitcast.11), custom_call_target="tpu_custom_call" | custom-call | tf_op jit(solution)/shard_map/pallas_call | solution.py:230
  50.5 0.7 %copy.7 = f32[1,1,1,768,128]{4,3,2,1,0:T(8,128)} copy(f32[1,1,1,768,128]{4,3,2,1,0:T(8,128)S(1)} %bitcast.6) | data formatting | bytes 786432
Async XLA Ops:
  1.4 1.3 %copy-start = (bf16[1,1,1,768,768]{4,3,2,1,0:T(8,128)(2,1)S(1)}, bf16[1,1,1,768,768]{4,3,2,1,0:T(8,128)(2,1)}, u32[]{:S(2)}) copy-start(bf16[1,1,1,768,768]{4,3,2,1,0:T(8,128)(2,1)} %param.6) | copy-start | bytes 3538948
  2.7 1.3 %copy-start.1 = (bf16[1,1,1,768,768]{4,3,2,1,0:T(8,128)(2,1)S(1)}, bf16[1,1,1,768,768]{4,3,2,1,0:T(8,128)(2,1)}, u32[]{:S(2)}) copy-start(bf16[1,1,1,768,768]{4,3,2,1,0:T(8,128)(2,1)} %param.7) | copy-start | bytes 3538948
  3.9 0.9 %copy-start.2 = (bf16[1,1,1,768,128]{4,3,2,1,0:T(8,128)(2,1)S(1)}, bf16[1,1,1,768,128]{4,3,2,1,0:T(8,128)(2,1)}, u32[]{:S(2)}) copy-start(bf16[1,1,1,768,128]{4,3,2,1,0:T(8,128)(2,1)} %param.5) | copy-start | bytes 589828

commit v2 on v1

--- a/solution.py
+++ b/solution.py
@@ -1,4 +1,5 @@
 import functools
+import math
 
 import jax
 import jax.numpy as jnp
@@ -9,7 +10,8 @@
 
 ITERS = 3
 AXES = ("gx", "gy", "gz")
-STAGES = ("gz", "gy", "gx")
+STAGES = (("gz",), ("gx", "gy"))
+GROUP = 2
 MESH = pl.DeviceIdType.MESH
 F32 = jnp.float32
 BF16 = jnp.bfloat16
@@ -19,19 +21,36 @@
     return jnp.dot(a, b, preferred_element_type=F32)
 
 
-def kernel(sizes, disp, flex, schur, rows, mult, out, table, picks, wpicks, temp,
+def kernel(sizes, disp_in, flex_in, schur_in, rows, mult, out_ref, disp, flex, schur, table, picks, wpicks, temp,
            op_a, op_b, send, recv, res, smo, img, along, across, way, vec, red_out, red_in,
-           send_sem, recv_sem, red_send_sem, red_recv_sem):
+           load_sem, send_sem, recv_sem, red_send_sem, red_recv_sem):
+    loads_in = [pltpu.make_async_copy(a.at[0, 0, 0], b, load_sem.at[i])
+                for i, (a, b) in enumerate(((disp_in, disp), (schur_in, schur), (flex_in, flex)))]
+    for copy in loads_in:
+        copy.start()
     width, loads = disp.shape
-    faces, length = rows.shape
-    slots = faces * length
+    slots = rows.shape[-1]
+    faces = 6
+    length = slots // faces
+    out = out_ref.at[0, 0, 0]
     index = {a: lax.axis_index(a) for a in AXES}
     barrier = pltpu.get_barrier_semaphore()
+
+    def count(s):
+        return math.prod(sizes[a] for a in STAGES[s])
+
+    def peer(s, d):
+        if len(STAGES[s]) == 1:
+            a = STAGES[s][0]
+            return {a: lax.rem(index[a] + d, sizes[a])}
+        a, b = STAGES[s]
+        place = lax.rem(index[a] * sizes[b] + index[b] + d, count(s))
+        return {a: place // sizes[b], b: lax.rem(place, sizes[b])}
+
     peers = 0
-    for a in AXES:
-        for d in range(1, sizes[a]):
-            pl.semaphore_signal(barrier, inc=1, device_id={a: lax.rem(index[a] + d, sizes[a])},
-                                device_id_type=MESH)
+    for s in range(len(STAGES)):
+        for d in range(1, count(s)):
+            pl.semaphore_signal(barrier, inc=1, device_id=peer(s, d), device_id_type=MESH)
             peers += 1
 
     have, toward = [], []
@@ -74,21 +93,27 @@
             face_arrival(e, f).wait_recv()
         return send[e, f].astype(F32) - recv[e, f].astype(F32)
 
+    def apply(op, vector, take):
+        x = vector[...]
+        for g in range(0, faces, GROUP):
+            y = dot(op[g * length:(g + GROUP) * length, :], x)
+            for f in range(g, g + GROUP):
+                take(f, y[block(f - g), :])
+
     def red_copy(k, s, d):
-        a = STAGES[s]
         return pltpu.make_async_remote_copy(
             src_ref=red_out.at[k, s], dst_ref=red_in.at[k, s, d - 1],
             send_sem=red_send_sem.at[k, s, d - 1], recv_sem=red_recv_sem.at[k, s, d - 1],
-            device_id={a: lax.rem(index[a] + d, sizes[a])}, device_id_type=MESH)
+            device_id=peer(s, d), device_id_type=MESH)
 
     def red_start(k, s, value):
         red_out[k, s] = value
-        for d in range(1, sizes[STAGES[s]]):
+        for d in range(1, count(s)):
             red_copy(k, s, d).start()
 
     def red_finish(k, s):
         total = red_out[k, s]
-        for d in range(1, sizes[STAGES[s]]):
+        for d in range(1, count(s)):
             red_copy(k, s, d).wait_recv()
             total = total + red_in[k, s, d - 1]
         return total
@@ -103,8 +128,8 @@
     lanes = lax.broadcasted_iota(jnp.int32, (length, length), 1)
     lines = lax.broadcasted_iota(jnp.int32, (length, length), 0)
     for f in range(faces):
-        row = jnp.broadcast_to(rows[f:f + 1, :], (length, length))
-        weight = jnp.broadcast_to(2.0 / mult[f:f + 1, :].astype(F32), (length, length))
+        row = jnp.broadcast_to(rows[0, 0, :, block(f)], (length, length))
+        weight = jnp.broadcast_to(2.0 / mult[0, 0, :, block(f)].astype(F32), (length, length))
         row_t = row.astype(F32).T.astype(jnp.int32)
         weight_t = weight.T
         for c in range(width // length):
@@ -114,34 +139,30 @@
             wpicks[block(f), block(c)] = jnp.where(hit, weight_t, 0.0).astype(BF16)
 
     pl.semaphore_wait(barrier, peers)
-    moved = disp[...]
-    for f in range(faces):
-        post(0, f, dot(picks[block(f), :], moved))
+    loads_in[0].wait()
+    apply(picks, disp, lambda f, y: post(0, f, y))
 
     def gather(left, op, scale, result):
-        @pl.loop(0, width // length)
-        def _(i):
-            part = pl.ds(pl.multiple_of(i * length, length), length)
-            temp[part, :] = dot(op[part, :], table[...]).astype(BF16)
-
-        @pl.loop(0, faces)
-        def _(i):
-            part = pl.ds(pl.multiple_of(i * length, length), length)
-            value = dot(left[part, :], temp[...])
+        for i in range(faces // 2):
+            part = slice(2 * i * length, 2 * (i + 1) * length)
+            temp[:, part] = dot(op[...], table[:, part]).astype(BF16)
+        for i in range(faces // 2):
+            part = slice(2 * i * length, 2 * (i + 1) * length)
+            value = dot(left[...], temp[:, part])
             if scale is not None:
-                value = value * scale
-            result[part, :] = value.astype(BF16)
-
-    weight_row = jnp.concatenate([2.0 / mult[f:f + 1, :].astype(F32) for f in range(faces)], axis=1)
+                value = value * scale[:, part]
+            result[:, part] = value.astype(BF16)
+
+    weight_row = 2.0 / mult[0, 0].astype(F32)
+    loads_in[1].wait()
     gather(wpicks, schur, weight_row, op_b)
 
     for f in range(faces):
         value = jumped(0, f)
         res[block(f), :] = value
         vec[block(f), :] = value.astype(BF16)
-    x = vec[...]
-    for f in range(faces):
-        post(1, f, dot(op_b[block(f), :], x))
+    apply(op_b, vec, lambda f, y: post(1, f, y))
+    loads_in[2].wait()
     gather(picks, flex, None, op_a)
     rho = jnp.zeros((1, loads), F32)
     for f in range(faces):
@@ -154,28 +175,25 @@
     for k in range(ITERS):
         last = k + 1 == ITERS
         e = 2 + 2 * k
-        x = vec[...]
-        curve = jnp.zeros((1, loads), F32)
-        for f in range(faces):
-            y = dot(op_a[block(f), :], x)
+        parts = []
+
+        def energy(f, y):
             if not last:
                 post(e, f, y)
-            curve = curve + total_of(smo[block(f), :] * y)
-        red_start(k, 0, pair(rho, curve))
+            parts.append(total_of(smo[block(f), :] * y))
+
+        apply(op_a, vec, energy)
+        red_start(k, 0, pair(rho, sum(parts)))
         if last:
             red_start(k, 1, red_finish(k, 0))
-            red_start(k, 2, red_finish(k, 1))
         else:
             for f in range(faces):
                 value = jumped(e, f)
                 img[block(f), :] = value
                 vec[block(f), :] = value.astype(BF16)
             red_start(k, 1, red_finish(k, 0))
-            x = vec[...]
-            for f in range(faces):
-                post(e + 1, f, dot(op_b[block(f), :], x))
-            red_start(k, 2, red_finish(k, 1))
-        sums = red_finish(k, 2)
+            apply(op_b, vec, lambda f, y: post(e + 1, f, y))
+        sums = red_finish(k, 1)
         rho_now, curve = sums[0:1, :], sums[1:2, :]
         if k == 0:
             beta = None
@@ -214,7 +232,7 @@
                 face_copy(e, f).wait_send()
     for k in range(ITERS):
         for s in range(len(STAGES)):
-            for d in range(1, sizes[STAGES[s]]):
+            for d in range(1, count(s)):
                 red_copy(k, s, d).wait_send()
 
 
@@ -224,15 +242,19 @@
     slots = face_rows.shape[-1]
     length = slots // 6
     exchanges = 2 * ITERS
-    most = max(max(sizes.values()) - 1, 1)
+    most = max(math.prod(sizes[a] for a in names) for names in STAGES)
+    stages = len(STAGES)
     vmem = pl.BlockSpec(memory_space=pltpu.VMEM)
     state = pltpu.VMEM((slots, loads), F32)
     result = pl.pallas_call(
         functools.partial(kernel, sizes),
-        out_shape=jax.ShapeDtypeStruct((slots, loads), F32),
-        in_specs=[vmem] * 5,
+        out_shape=jax.ShapeDtypeStruct((1, 1, 1, slots, loads), F32),
+        in_specs=[pl.BlockSpec(memory_space=pltpu.HBM)] * 3 + [vmem] * 2,
         out_specs=vmem,
         scratch_shapes=[
+            pltpu.VMEM((width, loads), BF16),
+            pltpu.VMEM((width, width), BF16),
+            pltpu.VMEM((width, width), BF16),
             pltpu.VMEM((width, slots), BF16),
             pltpu.VMEM((slots, width), BF16),
             pltpu.VMEM((slots, width), BF16),
@@ -243,23 +265,21 @@
             pltpu.VMEM((exchanges, 6, length, loads), BF16),
             state, state, state, state, state, state,
             pltpu.VMEM((slots, loads), BF16),
-            pltpu.VMEM((ITERS, 3, 8, loads), F32),
-            pltpu.VMEM((ITERS, 3, most, 8, loads), F32),
+            pltpu.VMEM((ITERS, stages, 8, loads), F32),
+            pltpu.VMEM((ITERS, stages, most, 8, loads), F32),
+            pltpu.SemaphoreType.DMA((3,)),
             pltpu.SemaphoreType.DMA((exchanges, 6)),
             pltpu.SemaphoreType.DMA((exchanges, 6)),
-            pltpu.SemaphoreType.DMA((ITERS, 3, most)),
-            pltpu.SemaphoreType.DMA((ITERS, 3, most)),
+            pltpu.SemaphoreType.DMA((ITERS, stages, most)),
+            pltpu.SemaphoreType.DMA((ITERS, stages, most)),
         ],
         compiler_params=pltpu.CompilerParams(
             collective_id=0, has_side_effects=True, vmem_limit_bytes=44 * 1024 * 1024),
     )(
-        displacement.reshape(width, loads),
-        flexibility.reshape(width, width),
-        schur.reshape(width, width),
-        face_rows.reshape(6, length),
-        multiplicity.reshape(6, length),
+        displacement, flexibility, schur,
+        face_rows.reshape(1, 1, 1, slots), multiplicity.reshape(1, 1, 1, slots),
     )
-    return result.reshape(1, 1, 1, slots, loads)
+    return result
 
 
 def solution(mesh):

time: 51.5 us -> 45.6 us (0.89)
  Pallas kernels: 45.6 us -> 39.7 us
  other arithmetic: 1.4 us -> 0 us
  local copies, waits for them, and re-layouts: 4.21 us -> 5.58 us
    pallas_call x1, Pallas kernels: 45.6 us -> 39.7 us  [shards(): pl.pallas_call(functools.partial(kernel, sizes), out_shape=jax.ShapeDtype...]
    unnamed x2 -> x0, other arithmetic: 1.4 us -> none
    unnamed x7 -> x11, local copies, waits for them, and re-layouts: 4.21 us -> 5.58 us
where the time goes in v2:
time: 45.6 us; the launch traced here: 45.3 us
  Pallas kernels  39.7 us (87%)
  local copies, waits for them, and re-layouts  5.58 us (12%)
    pallas_call x1, Pallas kernels, shards(): pl.pallas_call(functools.partial(kernel, sizes), out_shape=jax.ShapeDtype...  39.7 us
    unnamed x11, local copies, waits for them, and re-layouts  5.58 us

profile of v2, /device:TPU:0, one launch (start us, length us, event | category | flops | bytes accessed | tf_op | source)
XLA Modules:
  0.0 45.3 jit_solution(14843301722492161453)
XLA Ops:
  0.0 0.0 copy-start
  0.0 1.3 %copy-done = bf16[1,1,1,768,768]{4,3,2,1,0:T(8,128)(2,1)S(1)} copy-done((bf16[1,1,1,768,768]{4,3,2,1,0:T(8,128)(2,1)S(1)}, bf16[1,1,1,768,768]{4,3,2,1,0:T(8,128)(2,1)}, u32[]{:S(2)}) %copy-start) | copy-done | bytes 1179672
  1.3 0.0 copy-start.1
  1.3 1.3 %copy-done.1 = bf16[1,1,1,768,768]{4,3,2,1,0:T(8,128)(2,1)S(1)} copy-done((bf16[1,1,1,768,768]{4,3,2,1,0:T(8,128)(2,1)S(1)}, bf16[1,1,1,768,768]{4,3,2,1,0:T(8,128)(2,1)}, u32[]{:S(2)}) %copy-start.1) | copy-done | bytes 1179672
  2.5 0.0 copy-start.2
  2.5 0.9 %copy-done.2 = bf16[1,1,1,768,128]{4,3,2,1,0:T(8,128)(2,1)S(1)} copy-done((bf16[1,1,1,768,128]{4,3,2,1,0:T(8,128)(2,1)S(1)}, bf16[1,1,1,768,128]{4,3,2,1,0:T(8,128)(2,1)}, u32[]{:S(2)}) %copy-start.2) | copy-done | bytes 196632
  3.5 0.0 copy-start.3
  3.5 0.7 %copy-done.3 = s32[1,1,1,768]{3,2,1,0:T(1,128)S(1)} copy-done((s32[1,1,1,768]{3,2,1,0:T(1,128)S(1)}, s32[1,1,1,768]{3,2,1,0:T(1,128)}, u32[]{:S(2)}) %copy-start.3) | copy-done | bytes 3096
  4.2 0.0 copy-start.4
  4.2 0.7 %copy-done.4 = s32[1,1,1,768]{3,2,1,0:T(1,128)S(1)} copy-done((s32[1,1,1,768]{3,2,1,0:T(1,128)S(1)}, s32[1,1,1,768]{3,2,1,0:T(1,128)}, u32[]{:S(2)}) %copy-start.4) | copy-done | bytes 3096
  4.8 39.7 %shard_map.55 = f32[1,1,1,768,128]{4,3,2,1,0:T(8,128)S(1)} custom-call(bf16[1,1,1,768,128]{4,3,2,1,0:T(8,128)(2,1)S(1)} %copy-done.2, bf16[1,1,1,768,768]{4,3,2,1,0:T(8,128)(2,1)S(1)} %copy-done, bf16[1,1,1,768,768]{4,3,2,1,0:T(8,128)(2,1)S(1)} %copy-done.1, s32[1,1,1,768]{3,2,1,0:T(1,128)S(1)} %copy-done.3, s32[1,1,1,768]{3,2,1,0:T(1,128)S(1)} %copy-done.4), custom_call_target="tpu_custom_call" | custom-call | tf_op jit(solution)/shard_map/pallas_call | solution.py:249
  44.6 0.7 %copy.7 = f32[1,1,1,768,128]{4,3,2,1,0:T(8,128)} copy(f32[1,1,1,768,128]{4,3,2,1,0:T(8,128)S(1)} %shard_map.55) | data formatting | bytes 786432
Async XLA Ops:
  0.0 1.3 %copy-start = (bf16[1,1,1,768,768]{4,3,2,1,0:T(8,128)(2,1)S(1)}, bf16[1,1,1,768,768]{4,3,2,1,0:T(8,128)(2,1)}, u32[]{:S(2)}) copy-start(bf16[1,1,1,768,768]{4,3,2,1,0:T(8,128)(2,1)} %flex_in.1) | copy-start | bytes 3538948
  1.3 1.3 %copy-start.1 = (bf16[1,1,1,768,768]{4,3,2,1,0:T(8,128)(2,1)S(1)}, bf16[1,1,1,768,768]{4,3,2,1,0:T(8,128)(2,1)}, u32[]{:S(2)}) copy-start(bf16[1,1,1,768,768]{4,3,2,1,0:T(8,128)(2,1)} %schur_in.1) | copy-start | bytes 3538948
  2.5 0.9 %copy-start.2 = (bf16[1,1,1,768,128]{4,3,2,1,0:T(8,128)(2,1)S(1)}, bf16[1,1,1,768,128]{4,3,2,1,0:T(8,128)(2,1)}, u32[]{:S(2)}) copy-start(bf16[1,1,1,768,128]{4,3,2,1,0:T(8,128)(2,1)} %disp_in.1) | copy-start | bytes 589828
  3.5 0.7 %copy-start.3 = (s32[1,1,1,768]{3,2,1,0:T(1,128)S(1)}, s32[1,1,1,768]{3,2,1,0:T(1,128)}, u32[]{:S(2)}) copy-start(s32[1,1,1,768]{3,2,1,0:T(1,128)} %rows.1) | copy-start | bytes 9220
  4.2 0.7 %copy-start.4 = (s32[1,1,1,768]{3,2,1,0:T(1,128)S(1)}, s32[1,1,1,768]{3,2,1,0:T(1,128)}, u32[]{:S(2)}) copy-start(s32[1,1,1,768]{3,2,1,0:T(1,128)} %mult.1) | copy-start | bytes 9220

commit v3 on v2

--- a/solution.py
+++ b/solution.py
@@ -12,6 +12,7 @@
 AXES = ("gx", "gy", "gz")
 STAGES = (("gz",), ("gx", "gy"))
 GROUP = 2
+ARRIVE = (4, 5, 2, 3, 0, 1)
 MESH = pl.DeviceIdType.MESH
 F32 = jnp.float32
 BF16 = jnp.bfloat16
@@ -21,12 +22,15 @@
     return jnp.dot(a, b, preferred_element_type=F32)
 
 
-def kernel(sizes, disp_in, flex_in, schur_in, rows, mult, out_ref, disp, flex, schur, table, picks, wpicks, temp,
+def kernel(sizes, disp_in, flex_in, schur_in, rows_in, mult_in, out_ref, disp, flex, schur,
+           rows, mult, table, picks, wpicks, temp,
            op_a, op_b, send, recv, res, smo, img, along, across, way, vec, red_out, red_in,
            load_sem, send_sem, recv_sem, red_send_sem, red_recv_sem):
+    lists_in = [pltpu.make_async_copy(rows_in, rows, load_sem.at[3]),
+                pltpu.make_async_copy(mult_in, mult, load_sem.at[4])]
     loads_in = [pltpu.make_async_copy(a.at[0, 0, 0], b, load_sem.at[i])
                 for i, (a, b) in enumerate(((disp_in, disp), (schur_in, schur), (flex_in, flex)))]
-    for copy in loads_in:
+    for copy in lists_in + loads_in:
         copy.start()
     width, loads = disp.shape
     slots = rows.shape[-1]
@@ -125,6 +129,8 @@
     def total_of(value):
         return jnp.sum(value, axis=0, keepdims=True)
 
+    for copy in lists_in:
+        copy.wait()
     lanes = lax.broadcasted_iota(jnp.int32, (length, length), 1)
     lines = lax.broadcasted_iota(jnp.int32, (length, length), 0)
     for f in range(faces):
@@ -157,7 +163,7 @@
     loads_in[1].wait()
     gather(wpicks, schur, weight_row, op_b)
 
-    for f in range(faces):
+    for f in ARRIVE:
         value = jumped(0, f)
         res[block(f), :] = value
         vec[block(f), :] = value.astype(BF16)
@@ -165,7 +171,7 @@
     loads_in[2].wait()
     gather(picks, flex, None, op_a)
     rho = jnp.zeros((1, loads), F32)
-    for f in range(faces):
+    for f in ARRIVE:
         value = jumped(1, f)
         smo[block(f), :] = value
         vec[block(f), :] = value.astype(BF16)
@@ -187,7 +193,7 @@
         if last:
             red_start(k, 1, red_finish(k, 0))
         else:
-            for f in range(faces):
+            for f in ARRIVE:
                 value = jumped(e, f)
                 img[block(f), :] = value
                 vec[block(f), :] = value.astype(BF16)
@@ -203,7 +209,7 @@
             alpha = rho_now / (curve - beta * rho_now / alpha)
         rho_old = rho_now
         rho = jnp.zeros((1, loads), F32)
-        for f in range(faces):
+        for f in ARRIVE:
             b = block(f)
             p = smo[b, :] if beta is None else smo[b, :] + beta * way[b, :]
             total = alpha * p if beta is None else out[b, :] + alpha * p
@@ -249,12 +255,14 @@
     result = pl.pallas_call(
         functools.partial(kernel, sizes),
         out_shape=jax.ShapeDtypeStruct((1, 1, 1, slots, loads), F32),
-        in_specs=[pl.BlockSpec(memory_space=pltpu.HBM)] * 3 + [vmem] * 2,
+        in_specs=[pl.BlockSpec(memory_space=pltpu.HBM)] * 5,
         out_specs=vmem,
         scratch_shapes=[
             pltpu.VMEM((width, loads), BF16),
             pltpu.VMEM((width, width), BF16),
             pltpu.VMEM((width, width), BF16),
+            pltpu.VMEM((1, 1, 1, slots), jnp.int32),
+            pltpu.VMEM((1, 1, 1, slots), jnp.int32),
             pltpu.VMEM((width, slots), BF16),
             pltpu.VMEM((slots, width), BF16),
             pltpu.VMEM((slots, width), BF16),
@@ -267,14 +275,14 @@
             pltpu.VMEM((slots, loads), BF16),
             pltpu.VMEM((ITERS, stages, 8, loads), F32),
             pltpu.VMEM((ITERS, stages, most, 8, loads), F32),
-            pltpu.SemaphoreType.DMA((3,)),
+            pltpu.SemaphoreType.DMA((5,)),
             pltpu.SemaphoreType.DMA((exchanges, 6)),
             pltpu.SemaphoreType.DMA((exchanges, 6)),
             pltpu.SemaphoreType.DMA((ITERS, stages, most)),
             pltpu.SemaphoreType.DMA((ITERS, stages, most)),
         ],
         compiler_params=pltpu.CompilerParams(
-            collective_id=0, has_side_effects=True, vmem_limit_bytes=44 * 1024 * 1024),
+            collective_id=0, has_side_effects=True, vmem_limit_bytes=63 * 1024 * 1024),
     )(
         displacement, flexibility, schur,
         face_rows.reshape(1, 1, 1, slots), multiplicity.reshape(1, 1, 1, slots),

time: 45.6 us -> 41.5 us (0.910)
  local copies, waits for them, and re-layouts: 5.58 us -> 1.77 us
    unnamed x11 -> x1, local copies, waits for them, and re-layouts: 5.58 us -> 1.77 us
where the time goes in v3:
time: 41.5 us; the launch traced here: 41.4 us
  Pallas kernels  39.6 us (95%)
  local copies, waits for them, and re-layouts  1.77 us (4%)
    pallas_call x1, Pallas kernels, shards(): pl.pallas_call(functools.partial(kernel, sizes), out_shape=jax.ShapeDtype...  39.6 us
    unnamed x1, local copies, waits for them, and re-layouts  1.77 us

profile of v3, /device:TPU:0, one launch (start us, length us, event | category | flops | bytes accessed | tf_op | source)
XLA Modules:
  0.0 41.4 jit_solution(14623543393120918261)
XLA Ops:
  0.0 39.6 %shard_map.55 = f32[1,1,1,768,128]{4,3,2,1,0:T(8,128)} custom-call(bf16[1,1,1,768,128]{4,3,2,1,0:T(8,128)(2,1)} %disp_in.1, bf16[1,1,1,768,768]{4,3,2,1,0:T(8,128)(2,1)} %flex_in.1, bf16[1,1,1,768,768]{4,3,2,1,0:T(8,128)(2,1)} %schur_in.1, s32[1,1,1,768]{3,2,1,0:T(1,128)} %rows_in.1, s32[1,1,1,768]{3,2,1,0:T(1,128)} %mult_in.1), custom_call_target="tpu_custom_call" | custom-call | tf_op jit(solution)/shard_map/pallas_call | solution.py:255
  39.6 1.8 %copy.7 = f32[1,1,1,768,128]{4,3,2,1,0:T(8,128)} copy(f32[1,1,1,768,128]{4,3,2,1,0:T(8,128)} %shard_map.55) | data formatting | bytes 786432

commit v4 on v3

--- a/solution.py
+++ b/solution.py
@@ -11,7 +11,7 @@
 ITERS = 3
 AXES = ("gx", "gy", "gz")
 STAGES = (("gz",), ("gx", "gy"))
-GROUP = 2
+GROUPS = ((0, 1), (1, 2), (2, 4), (4, 6))
 ARRIVE = (4, 5, 2, 3, 0, 1)
 MESH = pl.DeviceIdType.MESH
 F32 = jnp.float32
@@ -99,9 +99,9 @@
 
     def apply(op, vector, take):
         x = vector[...]
-        for g in range(0, faces, GROUP):
-            y = dot(op[g * length:(g + GROUP) * length, :], x)
-            for f in range(g, g + GROUP):
+        for g, end in GROUPS:
+            y = dot(op[g * length:end * length, :], x)
+            for f in range(g, end):
                 take(f, y[block(f - g), :])
 
     def red_copy(k, s, d):

time: 41.5 us -> 41.6 us (level)
  no operation moved by 1% of the time
where the time goes in v4:
time: 41.6 us; the launch traced here: 41.5 us
  Pallas kernels  39.7 us (95%)
  local copies, waits for them, and re-layouts  1.77 us (4%)
    pallas_call x1, Pallas kernels, shards(): pl.pallas_call(functools.partial(kernel, sizes), out_shape=jax.ShapeDtype...  39.7 us
    unnamed x1, local copies, waits for them, and re-layouts  1.77 us

profile of v4, /device:TPU:0, one launch (start us, length us, event | category | flops | bytes accessed | tf_op | source)
XLA Modules:
  0.0 41.5 jit_solution(15611756771279763469)
XLA Ops:
  0.0 39.7 %shard_map.55 = f32[1,1,1,768,128]{4,3,2,1,0:T(8,128)} custom-call(bf16[1,1,1,768,128]{4,3,2,1,0:T(8,128)(2,1)} %disp_in.1, bf16[1,1,1,768,768]{4,3,2,1,0:T(8,128)(2,1)} %flex_in.1, bf16[1,1,1,768,768]{4,3,2,1,0:T(8,128)(2,1)} %schur_in.1, s32[1,1,1,768]{3,2,1,0:T(1,128)} %rows_in.1, s32[1,1,1,768]{3,2,1,0:T(1,128)} %mult_in.1), custom_call_target="tpu_custom_call" | custom-call | tf_op jit(solution)/shard_map/pallas_call | solution.py:255
  39.7 1.8 %copy.7 = f32[1,1,1,768,128]{4,3,2,1,0:T(8,128)} copy(f32[1,1,1,768,128]{4,3,2,1,0:T(8,128)} %shard_map.55) | data formatting | bytes 786432
